TPU v7x, 512 devices: a whole 4x8x8 slice. The times are simulated.
512 devices in a mesh: space: 16 (over z, core), member: 8 (over y), tm: 4 (over x).
Axes of the slice: x: 4, y: 8, z: 8, core: 2. Of those that a mesh axis runs over, the one named last changes fastest.
Arguments:
- ens_pert: bfloat16 [8, 128, 131072], P('tm', 'member', 'space'), may hold values from -6 to 6
- weights: float32 [128, 512], P('member', 'space'), may hold values from -6 to 6
- foot_block: int32 [8, 16, 16, 8, 32], P('tm', 'space'), may hold values from 0 to 31
- foot_offset: int32 [8, 16, 16, 8, 32], P('tm', 'space'), may hold values from 0 to 255
- innovation: float32 [8, 16, 8, 16, 32], P('tm', 'space', 'member'), may hold values from -6 to 6
- inv_var: float32 [8, 16, 8, 16, 32], P('tm', 'space', 'member'), may hold values from 0.25 to 2.5
- obs_count: int32 [8, 16, 8, 16], P('tm', 'space', 'member'), may hold values from 1 to 32, as said below
Outputs:
- gradient: float32 [128, 512], P('member', 'space')
Inputs may be any that keep to these rules, and one draw needn't show every extreme that they name: `obs_count`: live slots come first among the 32 slots; in every time slot one destination tile has all 32 slots live from every owner.
All inputs are finite; a program needn't handle non-finite values.
Results may differ from a plain program's by a relative error of at most 0.0029.
Values sent between devices are 32-bit elements; how exact they have to be, the bound alone decides.
No kernel may reach another device: no remote copies, remote signals or barrier semaphores. Data moves between devices by JAX's collectives and lax.ppermute only.
A program may use at most 64 MiB of HBM per device.

v0:
```python
import math
import jax
import jax.numpy as jnp
from jax import lax
from jax.sharding import PartitionSpec as P

BLOCK = 256


def split_pair(values, axis_at):
    upper = lax.optimization_barrier(values.astype(jnp.bfloat16))
    lower = (values - upper.astype(jnp.float32)).astype(jnp.bfloat16)
    return jnp.concatenate([upper, lower], axis=axis_at)


def shards(ens_pert, weights, foot_block, foot_offset, innovation, inv_var, obs_count):
    tile_count = lax.axis_size("space")
    group_count = lax.axis_size("member")
    slot_count, members, cell_dev = ens_pert.shape
    capacity = foot_block.shape[-1]
    blk_dev = cell_dev // BLOCK
    norm_scale = 1.0 / math.sqrt(members * group_count - 1)
    pert_blocks = ens_pert.reshape(slot_count, members, blk_dev, BLOCK)
    weights_rounded = weights.astype(jnp.bfloat16)
    partial_field = norm_scale * jnp.einsum(
        "tmbc,mb->tbc", pert_blocks, weights_rounded, preferred_element_type=jnp.float32
    )
    split_field = split_pair(partial_field, 1)
    block_rows = jnp.transpose(foot_block.reshape(slot_count, tile_count, -1), (1, 0, 2))
    offset_rows = jnp.transpose(foot_offset.reshape(slot_count, tile_count, -1), (1, 0, 2))
    block_iota = lax.broadcasted_iota(jnp.int32, (1, blk_dev, 1), 1)
    offset_iota = lax.broadcasted_iota(jnp.int32, (1, 1, BLOCK), 2)

    def pick_tile(pair):
        blk_ids, off_ids = pair
        off_hot = (off_ids[:, :, None] == offset_iota).astype(jnp.bfloat16)
        proj = jnp.einsum("tjc,tkc->tjk", split_field, off_hot, preferred_element_type=jnp.float32)
        value = proj[:, :blk_dev] + proj[:, blk_dev:]
        chosen = jnp.where(blk_ids[:, None, :] == block_iota, value, jnp.zeros_like(value))
        return jnp.sum(chosen, axis=1)

    picked = jnp.transpose(lax.map(pick_tile, (block_rows, offset_rows)), (1, 0, 2))
    arrived_vals = lax.all_to_all(
        picked.reshape(slot_count, tile_count * group_count, capacity),
        ("space", "member"),
        split_axis=1,
        concat_axis=1,
        tiled=True,
    )
    model_obs = jnp.sum(arrived_vals.reshape(slot_count, tile_count, group_count, capacity), axis=2)
    innov_local = innovation.reshape(slot_count, tile_count, capacity)
    obs_weight = inv_var.reshape(slot_count, tile_count, capacity)
    counts = obs_count.reshape(slot_count, tile_count, 1)
    is_live = lax.broadcasted_iota(jnp.int32, (slot_count, tile_count, capacity), 2) < counts
    residual = jnp.where(
        is_live, obs_weight * (model_obs - innov_local), jnp.zeros_like(innov_local)
    )
    residual = residual.reshape(slot_count, 1, 1, tile_count, capacity)
    spread = lax.all_gather(residual, "member", axis=2, tiled=True)
    arrived = lax.all_to_all(spread, "space", split_axis=3, concat_axis=1, tiled=True)
    arrived_rows = jnp.transpose(arrived.reshape(slot_count, tile_count, -1), (1, 0, 2))

    def add_tile(total, triple):
        blk_ids, off_ids, values = triple
        off_hot = (off_ids[:, :, None] == offset_iota).astype(jnp.bfloat16)
        placed = jnp.where(
            blk_ids[:, None, :] == block_iota, values[:, None, :], jnp.zeros((), jnp.float32)
        )
        both = split_pair(placed, 1)
        part_sum = jnp.einsum("tjk,tkc->tjc", both, off_hot, preferred_element_type=jnp.float32)
        return (total + (part_sum[:, :blk_dev] + part_sum[:, blk_dev:]), None)

    start_total = jnp.zeros((slot_count, blk_dev, BLOCK), jnp.float32)
    adjoint, _ = lax.scan(add_tile, start_total, (block_rows, offset_rows, arrived_rows))
    adjoint_rounded = adjoint.astype(jnp.bfloat16)
    local_grad = jnp.einsum(
        "tmbc,tbc->mb", pert_blocks, adjoint_rounded, preferred_element_type=jnp.float32
    )
    summed = lax.psum(local_grad, "tm")
    return weights + norm_scale * summed


def solution(mesh):
    in_specs = (
        P("tm", "member", "space"),
        P("member", "space"),
        P("tm", "space", None, None, None),
        P("tm", "space", None, None, None),
        P("tm", "space", "member", None, None),
        P("tm", "space", "member", None, None),
        P("tm", "space", "member", None),
    )
    out_specs = P("member", "space")
    return jax.shard_map(shards, mesh=mesh, in_specs=in_specs, out_specs=out_specs, check_vma=False)
```

profile of v0, /device:TPU:1, one launch (start us, length us, event | category | flops | bytes accessed | tf_op | source)
XLA Modules:
  0.0 95.3 jit_solution(16273810836954491873)
XLA Ops:
  0.0 0.7 convert_bitcast_fusion.1
  0.7 0.1 copy.38
  0.8 1.2 %fusion.21 = f32[32,1,2,256]{3,1,2,0:T(1,128)S(1)} fusion(bf16[16,32,1,1]{0,2,3,1:T(2,128)(2,1)S(1)} %copy.38, bf16[2,2,32,8,256]{4,3,2,1,0:T(8,128)(2,1)} %bitcast.84), kind=kOutput, calls=%fused_computation.32 | convolution fusion | flops 524288 | bytes 590848 | tf_op jit(solution)/shard_map/tmbc,mb->tbc/dot_general | solution.py:25
  2.1 0.0 copy-start.1
  2.1 0.8 copy-done.1
  3.0 0.1 reshape.52
  3.1 0.1 reshape.53
  3.2 0.1 copy_bitcast_fusion
  3.2 5.8 %while.22 = (s32[]{:T(128)}, f32[16,2,256]{2,1,0:T(2,128)S(1)}, s32[16,2,256]{2,1,0:T(2,128)S(1)}, s32[16,2,256]{2,1,0:T(2,128)S(1)}, bf16[2,64,256]{2,1,0:T(8,128)(2,1)S(1)}, /*index=5*/s32[]{:T(128)}) while((s32[]{:T(128)}, f32[16,2,256]{2,1,0:T(2,128)S(1)}, s32[16,2,256]{2,1,0:T(2,128)S(1)}, s32[16,2,256]{2,1,0:T(2,128)S(1)}, ...), condition=%wide.region_2.3_spmd.clone, body=%wide.region_0.2_spmd.clone.sunk | while | flops 16973312 | bytes 346189 | solution.py:42
  3.3 0.3 convolution_bitcast_fusion.2
  3.6 0.3 convolution_bitcast_fusion.2
  4.0 0.3 convolution_bitcast_fusion.2
  4.3 0.3 convolution_bitcast_fusion.2
  4.7 0.3 convolution_bitcast_fusion.2
  5.1 0.3 convolution_bitcast_fusion.2
  5.4 0.3 convolution_bitcast_fusion.2
  5.8 0.3 convolution_bitcast_fusion.2
  6.2 0.3 convolution_bitcast_fusion.2
  6.5 0.3 convolution_bitcast_fusion.2
  6.9 0.3 convolution_bitcast_fusion.2
  7.2 0.3 convolution_bitcast_fusion.2
  7.6 0.3 convolution_bitcast_fusion.2
  8.0 0.3 convolution_bitcast_fusion.2
  8.3 0.3 convolution_bitcast_fusion.2
  8.7 0.3 convolution_bitcast_fusion.2
  9.0 0.1 reshape.45
  9.1 0.8 copy.33
  9.9 18.4 %all-to-all-start = ((f32[2,128,32]{2,0,1:T(2,128)}), f32[2,128,32]{2,0,1:T(2,128)S(1)}, u32[]{:S(2)}, u32[]{:S(2)}) async-start(f32[2,128,32]{2,0,1:T(2,128)} %copy.33), calls=%async_computation | async-start | bytes 262144 | tf_op jit(solution)/shard_map/all_to_all | solution.py:43
  28.3 0.0 copy-start.6
  28.3 0.7 copy-done.6
  29.0 0.1 copy.30
  29.1 11.8 %all-to-all-done = f32[2,128,32]{2,0,1:T(2,128)S(1)} async-done(((f32[2,128,32]{2,0,1:T(2,128)}), f32[2,128,32]{2,0,1:T(2,128)S(1)}, u32[]{:S(2)}, u32[]{:S(2)}) %all-to-all-start) | async-done | bytes 32800 | tf_op jit(solution)/shard_map/all_to_all | solution.py:43
  40.9 0.1 compare_select_fusion
  41.0 18.2 %all_gather.3 = f32[2,1,8,16,32]{4,3,1,0,2:T(8,128)S(1)} all-gather(f32[2,1,1,16,32]{4,3,1,0,2:T(8,128)S(1)} %copy.36), channel_id=1, replica_groups=mesh['space'=16,'member'=8,'tm'=4] {'member'}, dimensions={2}, use_global_device_ids=true | all-gather | bytes 36864 | tf_op jit(solution)/shard_map/all_gather | solution.py:59
  59.3 0.1 copy.66
  59.4 0.7 reshape.54
  60.1 10.0 %all-to-all-start.1 = ((f32[16,1,512]{2,1,0:T(1,128)}), f32[16,1,512]{2,1,0:T(1,128)S(1)}, u32[]{:S(2)}, u32[]{:S(2)}) async-start(f32[16,1,512]{2,1,0:T(1,128)} %reshape.54), calls=%async_computation.1 | async-start | bytes 65536 | tf_op jit(solution)/shard_map/all_to_all | solution.py:60
  70.1 7.5 %all-to-all-done.1 = f32[16,1,512]{2,1,0:T(1,128)S(1)} async-done(((f32[16,1,512]{2,1,0:T(1,128)}), f32[16,1,512]{2,1,0:T(1,128)S(1)}, u32[]{:S(2)}, u32[]{:S(2)}) %all-to-all-start.1) | async-done | bytes 32800 | tf_op jit(solution)/shard_map/all_to_all | solution.py:60
  77.6 0.5 broadcast.27
  78.1 0.7 reduce
  78.8 0.1 reshape.55
  78.9 0.1 reshape.47
  79.0 0.0 copy-start
  79.0 6.6 %while.23 = (s32[]{:T(128)}, f32[2,32,256]{2,1,0:T(8,128)S(1)}, s32[16,2,256]{2,1,0:T(2,128)S(1)}, f32[16,2,256]{2,1,0:T(2,128)S(1)}, s32[16,2,256]{2,1,0:T(2,128)S(1)}, /*index=5*/s32[]{:T(128)}, s32[]{:T(128)}) while((s32[]{:T(128)}, f32[2,32,256]{2,1,0:T(8,128)S(1)}, s32[16,2,256]{2,1,0:T(2,128)S(1)}, ...), condition=%wide.region_5.6_spmd.clone, body=%wide.region_4.5_spmd.clone.sunk | while | flops 17203200 | bytes 579679 | solution.py:74
  79.1 0.3 fusion.40
  79.5 0.3 fusion.40
  80.0 0.3 fusion.40
  80.4 0.3 fusion.40
  80.8 0.3 fusion.40
  81.2 0.3 fusion.40
  81.6 0.3 fusion.40
  82.0 0.3 fusion.40
  82.4 0.3 fusion.40
  82.8 0.3 fusion.40
  83.2 0.3 fusion.40
  83.7 0.3 fusion.40
  84.1 0.3 fusion.40
  84.5 0.3 fusion.40
  84.9 0.3 fusion.40
  85.3 0.3 fusion.40
  85.7 0.3 fusion.19
  85.9 0.1 copy.42
  86.0 8.7 %psum.7 = f32[16,32]{1,0:T(8,128)S(1)} all-reduce(f32[16,32]{1,0:T(8,128)S(1)} %bitcast.88), channel_id=1, replica_groups=mesh['space'=16,'member'=8,'tm'=4] {'tm'}, use_global_device_ids=true, to_apply=%region_6.7 | all-reduce | flops 512 | bytes 4096 | tf_op jit(solution)/shard_map/psum | solution.py:79
  94.7 0.6 multiply_add_fusion
  (147 shorter events, 2.1 us)
Async XLA Ops:
  2.1 0.9 copy-start.1
  2.1 1.0 %copy-start.2 = (s32[2,1,16,8,32]{4,3,2,1,0:T(8,128)S(1)}, s32[2,1,16,8,32]{4,3,2,1,0:T(8,128)}, u32[]{:S(2)}) copy-start(s32[2,1,16,8,32]{4,3,2,1,0:T(8,128)} %param.14) | copy-start | bytes 98308
  9.9 31.0 %all-to-all-start = ((f32[2,128,32]{2,0,1:T(2,128)}), f32[2,128,32]{2,0,1:T(2,128)S(1)}, u32[]{:S(2)}, u32[]{:S(2)}) async-start(f32[2,128,32]{2,0,1:T(2,128)} %copy.33), calls=%async_computation | async-start | bytes 262144 | tf_op jit(solution)/shard_map/all_to_all | solution.py:43
  28.3 0.7 copy-start.6
  29.1 11.8 %copy-start.4 = (f32[2,1,1,16,32]{4,3,2,1,0:T(8,128)S(1)}, f32[2,1,1,16,32]{4,3,2,1,0:T(8,128)}, u32[]{:S(2)}) copy-start(f32[2,1,1,16,32]{4,3,2,1,0:T(8,128)} %param.16) | copy-start | bytes 12292
  29.1 11.8 %copy-start.5 = (f32[2,1,1,16,32]{4,3,2,1,0:T(8,128)S(1)}, f32[2,1,1,16,32]{4,3,2,1,0:T(8,128)}, u32[]{:S(2)}) copy-start(f32[2,1,1,16,32]{4,3,2,1,0:T(8,128)} %param.15) | copy-start | bytes 12292
  60.1 17.5 %all-to-all-start.1 = ((f32[16,1,512]{2,1,0:T(1,128)}), f32[16,1,512]{2,1,0:T(1,128)S(1)}, u32[]{:S(2)}, u32[]{:S(2)}) async-start(f32[16,1,512]{2,1,0:T(1,128)} %reshape.54), calls=%async_computation.1 | async-start | bytes 65536 | tf_op jit(solution)/shard_map/all_to_all | solution.py:60
  79.0 6.6 %copy-start = (bf16[2,16,8192]{2,1,0:T(8,128)(2,1)S(1)}, bf16[2,16,8192]{2,1,0:T(8,128)(2,1)}, u32[]{:S(2)}) copy-start(bf16[2,16,8192]{2,1,0:T(8,128)(2,1)} %param.11) | copy-start | bytes 1572868
  86.0 8.7 %copy-start.3 = (f32[16,32]{1,0:T(8,128)S(1)}, f32[16,32]{1,0:T(8,128)}, u32[]{:S(2)}) copy-start(f32[16,32]{1,0:T(8,128)} %param.12) | copy-start | bytes 6148
where the time goes:
time: 95.7 us; the launch traced here: 95.3 us
  starting transfers between devices  28.4 us (30%)
  blocking collectives  26.9 us (28%)
  waiting for transfers between devices  19.2 us (20%)
  matrix products  10.3 us (11%)
  local copies, waits for them, and re-layouts  5.06 us (5%)
  other arithmetic  3.52 us (4%)
  loops' own time  1.59 us (2%)
    all_to_all x1, starting transfers between devices, shards(): lax.all_to_all(picked.reshape(slot_count, tile_count * group_count, capac...  18.4 us
    all_gather x1, blocking collectives, shards(): spread = lax.all_gather(residual, 'member', axis=2, tiled=True)  18.2 us
    all_to_all x1, waiting for transfers between devices, shards(): lax.all_to_all(picked.reshape(slot_count, tile_count * group_count, capac...  11.8 us
    all_to_all x1, starting transfers between devices, shards(): lax.all_to_all(spread, 'space', split_axis=3, concat_axis=1, tiled=True)  10 us
    psum x1, blocking collectives, shards(): summed = lax.psum(local_grad, 'tm')  8.7 us
    all_to_all x1, waiting for transfers between devices, shards(): lax.all_to_all(spread, 'space', split_axis=3, concat_axis=1, tiled=True)  7.48 us
    dot_general x16, matrix products, add_tile(): jnp.einsum('tjk,tkc->tjc', both, off_hot, preferred_element_type=jnp.floa...  4.45 us
    dot_general x16, matrix products, pick_tile(): jnp.einsum('tjc,tkc->tjk', split_field, off_hot, preferred_element_type=j...  4.35 us
  transfers between devices with their start and end apart: 2, of which 2 were waited for; matrix products, arithmetic and copies ran while one was open for 0% of the time, Pallas kernels for 0%

commit v1 on v0

--- a/solution.py
+++ b/solution.py
@@ -3,6 +3,7 @@
 import jax.numpy as jnp
 from jax import lax
 from jax.sharding import PartitionSpec as P
+from jax.lax import all_to_all, axis_size
 
 BLOCK = 256
 
@@ -56,7 +57,8 @@
         is_live, obs_weight * (model_obs - innov_local), jnp.zeros_like(innov_local)
     )
     residual = residual.reshape(slot_count, 1, 1, tile_count, capacity)
-    spread = lax.all_gather(residual, "member", axis=2, tiled=True)
+    out_arr = jnp.concatenate([residual for _ in range(axis_size("member"))], 2)
+    spread = all_to_all(out_arr, axis_name="member", split_axis=2, concat_axis=2, tiled=True)
     arrived = lax.all_to_all(spread, "space", split_axis=3, concat_axis=1, tiled=True)
     arrived_rows = jnp.transpose(arrived.reshape(slot_count, tile_count, -1), (1, 0, 2))
 

time: 95.7 us -> 83.1 us (0.87)
  blocking collectives: 26.9 us -> 17.9 us
  starting transfers between devices: 28.4 us -> 23.8 us
    all_gather x1 -> x0, blocking collectives: 18.2 us -> none  [shards(): spread = lax.all_gather(residual, 'member', axis=2, tiled=True)]
    all_to_all x0 -> x1, blocking collectives: none -> 9.25 us  [shards(): all_to_all(out_arr, axis_name='member', split_axis=2, concat_axis=2, tile...]
    all_to_all x1, starting transfers between devices: 10 us -> 5.34 us  [shards(): lax.all_to_all(spread, 'space', split_axis=3, concat_axis=1, tiled=True)]
    unnamed x16 -> x19, local copies, waits for them, and re-layouts: 2.36 us -> 2.71 us
where the time goes in v1:
time: 83.1 us; the launch traced here: 82.7 us
  starting transfers between devices  23.8 us (29%)
  waiting for transfers between devices  19.2 us (23%)
  blocking collectives  17.9 us (22%)
  matrix products  10.3 us (12%)
  local copies, waits for them, and re-layouts  5.4 us (6%)
  other arithmetic  4.19 us (5%)
  loops' own time  1.59 us (2%)
    all_to_all x1, starting transfers between devices, shards(): lax.all_to_all(picked.reshape(slot_count, tile_count * group_count, capac...  18.4 us
    all_to_all x1, waiting for transfers between devices, shards(): lax.all_to_all(picked.reshape(slot_count, tile_count * group_count, capac...  11.8 us
    all_to_all x1, blocking collectives, shards(): all_to_all(out_arr, axis_name='member', split_axis=2, concat_axis=2, tile...  9.25 us
    psum x1, blocking collectives, shards(): summed = lax.psum(local_grad, 'tm')  8.7 us
    all_to_all x1, waiting for transfers between devices, shards(): lax.all_to_all(spread, 'space', split_axis=3, concat_axis=1, tiled=True)  7.48 us
    all_to_all x1, starting transfers between devices, shards(): lax.all_to_all(spread, 'space', split_axis=3, concat_axis=1, tiled=True)  5.34 us
    dot_general x16, matrix products, add_tile(): jnp.einsum('tjk,tkc->tjc', both, off_hot, preferred_element_type=jnp.floa...  4.45 us
    dot_general x16, matrix products, pick_tile(): jnp.einsum('tjc,tkc->tjk', split_field, off_hot, preferred_element_type=j...  4.35 us
  transfers between devices with their start and end apart: 2, of which 2 were waited for; matrix products, arithmetic and copies ran while one was open for 0% of the time, Pallas kernels for 0%

profile of v1, /device:TPU:1, one launch (start us, length us, event | category | flops | bytes accessed | tf_op | source)
XLA Modules:
  0.0 82.7 jit_solution(5439320197923222274)
XLA Ops:
  0.0 0.7 convert_bitcast_fusion.1
  0.7 0.1 copy.29
  0.8 1.2 %fusion.21 = f32[32,1,2,256]{3,1,2,0:T(1,128)S(1)} fusion(bf16[16,32,1,1]{0,2,3,1:T(2,128)(2,1)S(1)} %copy.29, bf16[2,2,32,8,256]{4,3,2,1,0:T(8,128)(2,1)} %bitcast.89), kind=kOutput, calls=%fused_computation.32 | convolution fusion | flops 524288 | bytes 590848 | tf_op jit(solution)/shard_map/tmbc,mb->tbc/dot_general | solution.py:26
  2.1 0.8 %copy-done.1 = s32[2,1,16,8,32]{4,3,2,1,0:T(8,128)S(1)} copy-done((s32[2,1,16,8,32]{4,3,2,1,0:T(8,128)S(1)}, s32[2,1,16,8,32]{4,3,2,1,0:T(8,128)}, u32[]{:S(2)}) %copy-start.1) | copy-done | bytes 32792
  3.0 0.1 reshape.58
  3.1 0.1 reshape.59
  3.2 0.1 copy_bitcast_fusion
  3.2 5.8 %while.22 = (s32[]{:T(128)}, f32[16,2,256]{2,1,0:T(2,128)S(1)}, s32[16,2,256]{2,1,0:T(2,128)S(1)}, s32[16,2,256]{2,1,0:T(2,128)S(1)}, bf16[2,64,256]{2,1,0:T(8,128)(2,1)S(1)}, /*index=5*/s32[]{:T(128)}) while((s32[]{:T(128)}, f32[16,2,256]{2,1,0:T(2,128)S(1)}, s32[16,2,256]{2,1,0:T(2,128)S(1)}, s32[16,2,256]{2,1,0:T(2,128)S(1)}, ...), condition=%wide.region_2.3_spmd.clone, body=%wide.region_0.2_spmd.clone.sunk | while | flops 16973312 | bytes 346189 | solution.py:43
  3.3 0.3 convolution_bitcast_fusion.2
  3.6 0.3 convolution_bitcast_fusion.2
  4.0 0.3 convolution_bitcast_fusion.2
  4.3 0.3 convolution_bitcast_fusion.2
  4.7 0.3 convolution_bitcast_fusion.2
  5.1 0.3 convolution_bitcast_fusion.2
  5.4 0.3 convolution_bitcast_fusion.2
  5.8 0.3 convolution_bitcast_fusion.2
  6.2 0.3 convolution_bitcast_fusion.2
  6.5 0.3 convolution_bitcast_fusion.2
  6.9 0.3 convolution_bitcast_fusion.2
  7.2 0.3 convolution_bitcast_fusion.2
  7.6 0.3 convolution_bitcast_fusion.2
  8.0 0.3 convolution_bitcast_fusion.2
  8.3 0.3 convolution_bitcast_fusion.2
  8.7 0.3 convolution_bitcast_fusion.2
  9.0 0.1 reshape.50
  9.1 0.7 copy.25
  9.9 18.4 %all-to-all-start = ((f32[2,128,32]{2,0,1:T(2,128)}), f32[2,128,32]{2,0,1:T(2,128)S(1)}, u32[]{:S(2)}, u32[]{:S(2)}) async-start(f32[2,128,32]{2,0,1:T(2,128)} %copy.25), calls=%async_computation | async-start | bytes 262144 | tf_op jit(solution)/shard_map/all_to_all | solution.py:44
  28.3 0.7 copy-done.6
  29.0 0.1 copy.22
  29.1 11.8 %all-to-all-done = f32[2,128,32]{2,0,1:T(2,128)S(1)} async-done(((f32[2,128,32]{2,0,1:T(2,128)}), f32[2,128,32]{2,0,1:T(2,128)S(1)}, u32[]{:S(2)}, u32[]{:S(2)}) %all-to-all-start) | async-done | bytes 32800 | tf_op jit(solution)/shard_map/all_to_all | solution.py:44
  40.9 0.1 fusion.27
  41.1 0.2 reshape.60
  41.2 9.2 %all_to_all.25 = f32[8,1,1024]{2,1,0:T(1,128)S(1)} all-to-all(f32[8,1,1024]{2,1,0:T(1,128)S(1)} %reshape.60), channel_id=1, replica_groups=mesh['space'=16,'member'=8,'tm'=4] {'member'}, dimensions={0} | all-to-all | bytes 65536 | tf_op jit(solution)/shard_map/all_to_all | solution.py:61
  50.5 0.5 broadcast.29
  51.0 0.7 reduce
  51.7 0.2 reshape.61
  51.9 0.1 copy.57
  51.9 0.7 reshape.62
  52.7 5.3 %all-to-all-start.2 = ((f32[16,1,512]{2,1,0:T(1,128)}), f32[16,1,512]{2,1,0:T(1,128)S(1)}, u32[]{:S(2)}, u32[]{:S(2)}) async-start(f32[16,1,512]{2,1,0:T(1,128)} %reshape.62), calls=%async_computation.2 | async-start | bytes 65536 | tf_op jit(solution)/shard_map/all_to_all | solution.py:62
  58.0 7.5 %all-to-all-done.2 = f32[16,1,512]{2,1,0:T(1,128)S(1)} async-done(((f32[16,1,512]{2,1,0:T(1,128)}), f32[16,1,512]{2,1,0:T(1,128)S(1)}, u32[]{:S(2)}, u32[]{:S(2)}) %all-to-all-start.2) | async-done | bytes 32800 | tf_op jit(solution)/shard_map/all_to_all | solution.py:62
  65.5 0.7 reduce.1
  66.2 0.1 reshape.63
  66.3 0.1 reshape.53
  66.4 6.6 %while.23 = (s32[]{:T(128)}, f32[2,32,256]{2,1,0:T(8,128)S(1)}, s32[16,2,256]{2,1,0:T(2,128)S(1)}, f32[16,2,256]{2,1,0:T(2,128)S(1)}, s32[16,2,256]{2,1,0:T(2,128)S(1)}, /*index=5*/s32[]{:T(128)}, s32[]{:T(128)}) while((s32[]{:T(128)}, f32[2,32,256]{2,1,0:T(8,128)S(1)}, s32[16,2,256]{2,1,0:T(2,128)S(1)}, ...), condition=%wide.region_5.6_spmd.clone, body=%wide.region_4.5_spmd.clone.sunk | while | flops 17203200 | bytes 579679 | solution.py:76
  66.5 0.3 fusion.41
  66.9 0.3 fusion.41
  67.3 0.3 fusion.41
  67.7 0.3 fusion.41
  68.1 0.3 fusion.41
  68.6 0.3 fusion.41
  69.0 0.3 fusion.41
  69.4 0.3 fusion.41
  69.8 0.3 fusion.41
  70.2 0.3 fusion.41
  70.6 0.3 fusion.41
  71.0 0.3 fusion.41
  71.4 0.3 fusion.41
  71.9 0.3 fusion.41
  72.3 0.3 fusion.41
  72.7 0.3 fusion.41
  73.0 0.3 fusion.19
  73.3 0.1 copy.33
  73.4 8.7 %psum.7 = f32[16,32]{1,0:T(8,128)S(1)} all-reduce(f32[16,32]{1,0:T(8,128)S(1)} %bitcast.94), channel_id=1, replica_groups=mesh['space'=16,'member'=8,'tm'=4] {'tm'}, use_global_device_ids=true, to_apply=%region_6.7 | all-reduce | flops 512 | bytes 4096 | tf_op jit(solution)/shard_map/psum | solution.py:81
  82.1 0.6 multiply_add_fusion
  (150 shorter events, 2.2 us)
Async XLA Ops:
  2.1 0.9 %copy-start.1 = (s32[2,1,16,8,32]{4,3,2,1,0:T(8,128)S(1)}, s32[2,1,16,8,32]{4,3,2,1,0:T(8,128)}, u32[]{:S(2)}) copy-start(s32[2,1,16,8,32]{4,3,2,1,0:T(8,128)} %param.13) | copy-start | bytes 98308
  2.1 1.0 %copy-start.2 = (s32[2,1,16,8,32]{4,3,2,1,0:T(8,128)S(1)}, s32[2,1,16,8,32]{4,3,2,1,0:T(8,128)}, u32[]{:S(2)}) copy-start(s32[2,1,16,8,32]{4,3,2,1,0:T(8,128)} %param.14) | copy-start | bytes 98308
  9.9 31.0 %all-to-all-start = ((f32[2,128,32]{2,0,1:T(2,128)}), f32[2,128,32]{2,0,1:T(2,128)S(1)}, u32[]{:S(2)}, u32[]{:S(2)}) async-start(f32[2,128,32]{2,0,1:T(2,128)} %copy.25), calls=%async_computation | async-start | bytes 262144 | tf_op jit(solution)/shard_map/all_to_all | solution.py:44
  28.3 0.7 copy-start.6
  29.1 11.8 %copy-start.4 = (f32[2,1,1,16,32]{4,3,2,1,0:T(8,128)S(1)}, f32[2,1,1,16,32]{4,3,2,1,0:T(8,128)}, u32[]{:S(2)}) copy-start(f32[2,1,1,16,32]{4,3,2,1,0:T(8,128)} %param.16) | copy-start | bytes 12292
  29.1 11.8 %copy-start.5 = (f32[2,1,1,16,32]{4,3,2,1,0:T(8,128)S(1)}, f32[2,1,1,16,32]{4,3,2,1,0:T(8,128)}, u32[]{:S(2)}) copy-start(f32[2,1,1,16,32]{4,3,2,1,0:T(8,128)} %param.15) | copy-start | bytes 12292
  52.7 12.8 %all-to-all-start.2 = ((f32[16,1,512]{2,1,0:T(1,128)}), f32[16,1,512]{2,1,0:T(1,128)S(1)}, u32[]{:S(2)}, u32[]{:S(2)}) async-start(f32[16,1,512]{2,1,0:T(1,128)} %reshape.62), calls=%async_computation.2 | async-start | bytes 65536 | tf_op jit(solution)/shard_map/all_to_all | solution.py:62
  66.4 6.6 %copy-start = (bf16[2,16,8192]{2,1,0:T(8,128)(2,1)S(1)}, bf16[2,16,8192]{2,1,0:T(8,128)(2,1)}, u32[]{:S(2)}) copy-start(bf16[2,16,8192]{2,1,0:T(8,128)(2,1)} %param.11) | copy-start | bytes 1572868
  73.4 8.7 %copy-start.3 = (f32[16,32]{1,0:T(8,128)S(1)}, f32[16,32]{1,0:T(8,128)}, u32[]{:S(2)}) copy-start(f32[16,32]{1,0:T(8,128)} %param.12) | copy-start | bytes 6148
